TPU v7x, 32 devices: a whole 2x2x4 slice. The times are simulated.
32 devices in a mesh: px: 8 (over y, x, core), py: 4 (over z).
Axes of the slice: x: 2, y: 2, z: 4, core: 2. Of those that a mesh axis runs over, the one named last changes fastest.
Arguments:
- velocity: float32 [2, 64, 16, 1024], P(None, None, 'py', 'px'), may hold values from -15 to 15
- pressure: float32 [64, 16, 1024], P(None, 'py', 'px'), may hold values from -6 to 6
- mass: bfloat16 [64, 16, 1024], P(None, 'py', 'px'), may hold values from 0.049804688 to 0.5
- face_coeff: bfloat16 [2, 64, 16, 1024], P(None, None, 'py', 'px'), may hold values from 0.29882812 to 3
- vert_coeff: bfloat16 [63, 16, 1024], P(None, 'py', 'px'), may hold values from 1 to 20
- block_inverse: bfloat16 [4, 64, 16, 1024], P(None, None, 'py', 'px'), may hold values from -0.020019531 to 0.080078125
- orientation: int32 [2, 16, 1024], P(None, 'py', 'px'), may hold values from 0 to 1
Outputs:
- new_pressure: float32 [64, 16, 1024], P(None, 'py', 'px')
- new_velocity: float32 [2, 64, 16, 1024], P(None, None, 'py', 'px')
All inputs are finite; a program needn't handle non-finite values.
Results may differ from a plain program's by a relative error of at most 0.0003.
Values sent between devices are 32-bit elements; how exact they have to be, the bound alone decides.
A program may use at most 64 MiB of HBM per device.

v0:
```python
import jax
import jax.numpy as jnp
from jax import lax
from jax.sharding import PartitionSpec as P

BLOCK = 4
ITERS = 4
OUTER = 2


def extended(block, sides, width):
    for axis, dim in sides:
        count = lax.axis_size(axis)
        forward = [(i, i + 1) for i in range(count - 1)]
        forward.append((count - 1, 0))
        backward = [(target, source) for source, target in forward]
        low = lax.ppermute(
            lax.slice_in_dim(block, block.shape[dim] - width, None, axis=dim), axis, forward
        )
        high = lax.ppermute(lax.slice_in_dim(block, 0, width, axis=dim), axis, backward)
        block = jnp.concatenate([low, block, high], axis=dim)
    return block


def from_behind(value, axis, steps):
    count = lax.axis_size(axis)
    pairs = [(source, (source + steps) % count) for source in range(count)]
    return lax.ppermute(value, axis, pairs)


def from_behind_2(block, axis, distance):
    devices = range(lax.axis_size(axis))
    route = [(i - distance, i) for i in devices if i - distance in devices]
    return lax.ppermute(block, axis, route)


def rim(values):
    padded = extended(values, (("px", 2), ("py", 1)), 1)
    row_place = lax.axis_index("py")
    low_keep = (row_place > 0).astype(jnp.float32)
    high_keep = (row_place < lax.axis_size("py") - 1).astype(jnp.float32)
    padded = padded.at[:, 0, :].multiply(low_keep)
    return padded.at[:, -1, :].multiply(high_keep)


def operate(padded, mass, face_coeff, vert_coeff, west_pair, south_pair):
    values = padded[:, 1:-1, 1:-1]
    east_cell = padded[:, 1:-1, 2:]
    west_cell = padded[:, 1:-1, :-2]
    north_cell = padded[:, 2:, 1:-1]
    south_cell = padded[:, :-2, 1:-1]
    east_coef = face_coeff[0].astype(jnp.float32)
    north_coef = face_coeff[1].astype(jnp.float32)
    west_coef = jnp.concatenate([west_pair[1], east_coef[:, :, :-1]], axis=2)
    south_coef = jnp.concatenate([south_pair[1], north_coef[:, :-1, :]], axis=1)
    horizontal = (
        east_coef * (values - east_cell)
        + west_coef * (values - west_cell)
        + north_coef * (values - north_cell)
        + south_coef * (values - south_cell)
    )
    vert_coef = vert_coeff.astype(jnp.float32)
    upper_coef = jnp.pad(vert_coef, ((0, 1), (0, 0), (0, 0)))
    lower_coef = jnp.pad(vert_coef, ((1, 0), (0, 0), (0, 0)))
    above_cell = jnp.pad(values[1:], ((0, 1), (0, 0), (0, 0)))
    below_cell = jnp.pad(values[:-1], ((1, 0), (0, 0), (0, 0)))
    vertical = upper_coef * (values - above_cell) + lower_coef * (values - below_cell)
    return mass.astype(jnp.float32) * values + horizontal + vertical


def precondition(residual, block_inverse):
    block_count = residual.shape[0] // BLOCK
    blocks = residual.reshape((block_count, BLOCK) + residual.shape[1:])
    summed = jnp.zeros_like(blocks)
    for member in range(BLOCK):
        summed = (
            summed
            + block_inverse[member].astype(jnp.float32).reshape(blocks.shape)
            * blocks[:, member : member + 1]
        )
    return summed.reshape(residual.shape)


def seam_edges(flow, sign_flip, face_coeff):
    east_flux = sign_flip[0] * flow[0]
    north_flux = sign_flip[1] * flow[1]
    west_pair = from_behind(
        jnp.stack([east_flux[:, :, -1:], face_coeff[0][:, :, -1:].astype(jnp.float32)]), "px", 1
    )
    south_pair = from_behind_2(
        jnp.stack([north_flux[:, -1:, :], face_coeff[1][:, -1:, :].astype(jnp.float32)]), "py", 1
    )
    return (east_flux, north_flux, west_pair, south_pair)


def local(velocity, pressure, mass, face_coeff, vert_coeff, block_inverse, orientation):
    sign_flip = (2 * orientation - 1).astype(jnp.float32)
    current = pressure
    flow = velocity
    east_flux, north_flux, west_pair, south_pair = seam_edges(flow, sign_flip, face_coeff)
    padded_now = rim(current)
    for outer_step in range(OUTER):
        if outer_step > 0:
            east_flux, north_flux, west_pair, south_pair = seam_edges(flow, sign_flip, face_coeff)
        divergence = (
            east_flux
            - jnp.concatenate([west_pair[0], east_flux[:, :, :-1]], axis=2)
            + north_flux
            - jnp.concatenate([south_pair[0], north_flux[:, :-1, :]], axis=1)
        )
        right_side = mass.astype(jnp.float32) * current - divergence
        residual = right_side - operate(
            padded_now, mass, face_coeff, vert_coeff, west_pair, south_pair
        )
        searches = []
        images = []
        image_norms = []
        for inner_step in range(ITERS):
            search = precondition(residual, block_inverse)
            image = operate(rim(search), mass, face_coeff, vert_coeff, west_pair, south_pair)
            if inner_step > 0:
                projected = lax.psum(
                    jnp.stack([jnp.sum(image * images[member]) for member in range(inner_step)]),
                    ("px", "py"),
                )
                weights_proj = [
                    projected[member] / image_norms[member] for member in range(inner_step)
                ]
                for member in range(inner_step):
                    search = search - weights_proj[member] * searches[member]
                    image = image - weights_proj[member] * images[member]
            pair_sums = lax.psum(
                jnp.stack([jnp.sum(image * image), jnp.sum(residual * image)]), ("px", "py")
            )
            image_norm = pair_sums[0]
            step_size = pair_sums[1] / image_norm
            current = current + step_size * search
            residual = residual - step_size * image
            searches.append(search)
            images.append(image)
            image_norms.append(image_norm)
        padded_now = rim(current)
        east_cell = padded_now[:, 1:-1, 2:]
        north_cell = padded_now[:, 2:, 1:-1]
        flow = jnp.stack(
            [
                flow[0] + sign_flip[0] * face_coeff[0].astype(jnp.float32) * (current - east_cell),
                flow[1] + sign_flip[1] * face_coeff[1].astype(jnp.float32) * (current - north_cell),
            ]
        )
    return (current, flow)


def solution(mesh):
    placed = (
        P(None, None, "py", "px"),
        P(None, "py", "px"),
        P(None, "py", "px"),
        P(None, None, "py", "px"),
        P(None, "py", "px"),
        P(None, None, "py", "px"),
        P(None, "py", "px"),
    )
    return jax.shard_map(
        local,
        mesh=mesh,
        in_specs=placed,
        out_specs=(P(None, "py", "px"), P(None, None, "py", "px")),
        check_vma=False,
    )
```

profile of v0, /device:TPU:0, one launch (start us, length us, event | category | flops | bytes accessed | tf_op | source)
XLA Modules:
  0.0 787.3 jit_solution(6700544144653746193)
XLA Ops:
  2.2 2.9 collective-permute-start.3
  5.9 4.3 collective-permute-start.1
  22.3 2.6 collective-permute-done.6
  26.2 2.8 collective-permute-start.9
  28.9 2.7 collective-permute-done.8
  34.2 39.3 %psum.98 = f32[2]{0:T(128)S(1)} all-reduce(f32[2]{0:T(128)S(1)} %pad_maximum_fusion.53), channel_id=1, replica_groups=mesh['px'=8,'py'=4] {'px','py'}, use_global_device_ids=true, to_apply=%region_2.3 | all-reduce | flops 2 | bytes 16 | tf_op jit(solution)/shard_map/psum | solution.py:132
  91.0 39.3 %psum.99 = f32[1]{0:T(128)} all-reduce(f32[1]{0:T(128)} %bitcast.41), channel_id=1, replica_groups=mesh['px'=8,'py'=4] {'px','py'}, use_global_device_ids=true, to_apply=%region_4.5 | all-reduce | flops 1 | bytes 8 | tf_op jit(solution)/shard_map/psum | solution.py:122
  133.7 41.1 %psum.100 = f32[2]{0:T(128)S(1)} all-reduce(f32[2]{0:T(128)S(1)} %pad_maximum_fusion.54), channel_id=1, replica_groups=mesh['px'=8,'py'=4] {'px','py'}, use_global_device_ids=true, to_apply=%region_7.8 | all-reduce | flops 2 | bytes 16 | tf_op jit(solution)/shard_map/psum | solution.py:132
  179.7 2.6 collective-permute-done.14
  183.2 3.4 collective-permute-start.17
  191.5 39.5 %psum.101 = f32[2]{0:T(128)S(1)} all-reduce(f32[2]{0:T(128)S(1)} %pad_maximum_fusion.55), channel_id=1, replica_groups=mesh['px'=8,'py'=4] {'px','py'}, use_global_device_ids=true, to_apply=%region_10.11 | all-reduce | flops 2 | bytes 16 | tf_op jit(solution)/shard_map/psum | solution.py:122
  236.2 42.1 %psum.102 = f32[2]{0:T(128)S(1)} all-reduce(f32[2]{0:T(128)S(1)} %pad_maximum_fusion.56), channel_id=1, replica_groups=mesh['px'=8,'py'=4] {'px','py'}, use_global_device_ids=true, to_apply=%region_13.14 | all-reduce | flops 2 | bytes 16 | tf_op jit(solution)/shard_map/psum | solution.py:132
  283.3 2.7 collective-permute-done.18
  286.4 3.8 collective-permute-start.21
  295.7 39.7 %psum.103 = f32[3]{0:T(128)S(1)} all-reduce(f32[3]{0:T(128)S(1)} %pad_maximum_fusion.57), channel_id=1, replica_groups=mesh['px'=8,'py'=4] {'px','py'}, use_global_device_ids=true, to_apply=%region_17.18 | all-reduce | flops 3 | bytes 24 | tf_op jit(solution)/shard_map/psum | solution.py:122
  342.1 42.1 %psum.104 = f32[2]{0:T(128)S(1)} all-reduce(f32[2]{0:T(128)S(1)} %pad_maximum_fusion.58), channel_id=1, replica_groups=mesh['px'=8,'py'=4] {'px','py'}, use_global_device_ids=true, to_apply=%region_20.21 | all-reduce | flops 2 | bytes 16 | tf_op jit(solution)/shard_map/psum | solution.py:132
  388.9 2.7 collective-permute-done.22
  392.1 3.8 collective-permute-start.25
  407.4 3.7 collective-permute-done.28
  413.4 3.9 collective-permute-start.31
  422.3 39.5 %psum.105 = f32[2]{0:T(128)S(1)} all-reduce(f32[2]{0:T(128)S(1)} %pad_maximum_fusion.59), channel_id=1, replica_groups=mesh['px'=8,'py'=4] {'px','py'}, use_global_device_ids=true, to_apply=%region_23.24 | all-reduce | flops 2 | bytes 16 | tf_op jit(solution)/shard_map/psum | solution.py:132
  478.8 39.3 %psum.106 = f32[1]{0:T(128)} all-reduce(f32[1]{0:T(128)} %bitcast.107), channel_id=1, replica_groups=mesh['px'=8,'py'=4] {'px','py'}, use_global_device_ids=true, to_apply=%region_25.26 | all-reduce | flops 1 | bytes 8 | tf_op jit(solution)/shard_map/psum | solution.py:122
  521.4 41.4 %psum.107 = f32[2]{0:T(128)S(1)} all-reduce(f32[2]{0:T(128)S(1)} %pad_maximum_fusion.60), channel_id=1, replica_groups=mesh['px'=8,'py'=4] {'px','py'}, use_global_device_ids=true, to_apply=%region_28.29 | all-reduce | flops 2 | bytes 16 | tf_op jit(solution)/shard_map/psum | solution.py:132
  571.0 3.6 collective-permute-start.39
  579.5 39.5 %psum.108 = f32[2]{0:T(128)S(1)} all-reduce(f32[2]{0:T(128)S(1)} %pad_maximum_fusion.61), channel_id=1, replica_groups=mesh['px'=8,'py'=4] {'px','py'}, use_global_device_ids=true, to_apply=%region_31.32 | all-reduce | flops 2 | bytes 16 | tf_op jit(solution)/shard_map/psum | solution.py:122
  624.3 42.1 %psum.109 = f32[2]{0:T(128)S(1)} all-reduce(f32[2]{0:T(128)S(1)} %pad_maximum_fusion.62), channel_id=1, replica_groups=mesh['px'=8,'py'=4] {'px','py'}, use_global_device_ids=true, to_apply=%region_34.35 | all-reduce | flops 2 | bytes 16 | tf_op jit(solution)/shard_map/psum | solution.py:132
  671.3 2.7 collective-permute-done.40
  674.4 3.8 collective-permute-start.43
  683.7 39.5 %psum.110 = f32[3]{0:T(128)S(1)} all-reduce(f32[3]{0:T(128)S(1)} %pad_maximum_fusion.63), channel_id=1, replica_groups=mesh['px'=8,'py'=4] {'px','py'}, use_global_device_ids=true, to_apply=%region_38.39 | all-reduce | flops 3 | bytes 24 | tf_op jit(solution)/shard_map/psum | solution.py:122
  729.9 42.1 %psum.111 = f32[2]{0:T(128)S(1)} all-reduce(f32[2]{0:T(128)S(1)} %pad_maximum_fusion.64), channel_id=1, replica_groups=mesh['px'=8,'py'=4] {'px','py'}, use_global_device_ids=true, to_apply=%region_41.42 | all-reduce | flops 2 | bytes 16 | tf_op jit(solution)/shard_map/psum | solution.py:132
  776.8 2.7 collective-permute-done.44
  779.9 3.8 collective-permute-start.47
  (292 shorter events, 134.4 us)
Async XLA Ops:
  1.7 8.7 %collective-permute-start.2 = (f32[64,4,1]{2,0,1:T(8,128)S(1)}, f32[64,4,1]{2,0,1:T(8,128)S(1)}, u32[]{:S(2)}, u32[]{:S(2)}) collective-permute-start(f32[64,4,1]{2,0,1:T(8,128)S(1)} %get-tuple-element.434), channel_id=1, source_target_pairs={{0,4},{4,8},{8,12},{12,16},{16,20},{20,24},{24,28},{28,0},{1,5},{5... | collective-permute-start | bytes 3080 | tf_op jit(solution)/shard_map/ppermute | solution.py:17
  2.2 8.2 %collective-permute-start.3 = (f32[64,4,1]{2,0,1:T(8,128)S(1)}, f32[64,4,1]{2,0,1:T(8,128)S(1)}, u32[]{:S(2)}, u32[]{:S(2)}) collective-permute-start(f32[64,4,1]{2,0,1:T(8,128)S(1)} %get-tuple-element.435), channel_id=1, source_target_pairs={{4,0},{8,4},{12,8},{16,12},{20,16},{24,20},{28,24},{0,28},{5,1},{9... | collective-permute-start | bytes 3080 | tf_op jit(solution)/shard_map/ppermute | solution.py:20
  5.7 8.7 %collective-permute-start = (f32[2,64,4,1]{1,2,3,0:T(4,128)S(1)}, f32[2,64,4,1]{1,2,3,0:T(4,128)S(1)}, u32[]{:S(2)}, u32[]{:S(2)}) collective-permute-start(f32[2,64,4,1]{1,2,3,0:T(4,128)S(1)} %pad_maximum_fusion.52), channel_id=1, source_target_pairs={{0,4},{4,8},{8,12},{12,16},{16,20},{20,24},{24,28},{28,0},{1,5},{5... | collective-permute-start | bytes 6152 | tf_op jit(solution)/shard_map/ppermute | solution.py:28
  5.9 12.2 %collective-permute-start.1 = (f32[2,64,1,128]{3,1,2,0:T(8,128)S(1)}, f32[2,64,1,128]{3,1,2,0:T(8,128)S(1)}, u32[]{:S(2)}, u32[]{:S(2)}) collective-permute-start(f32[2,64,1,128]{3,1,2,0:T(8,128)S(1)} %pad_maximum_fusion.17), channel_id=1, source_target_pairs={{0,1},{1,2},{2,3},{4,5},{5,6},{6,7},{8,9},{9,10},{10,11},{12,13},{... | collective-permute-start | bytes 196616 | tf_op jit(solution)/shard_map/ppermute | solution.py:34
  10.5 6.7 collective-permute-start.4
  25.1 6.6 collective-permute-start.8
  75.9 5.6 collective-permute-start.11
  81.6 6.2 collective-permute-start.12
  83.8 6.0 collective-permute-start.13
  177.1 5.6 collective-permute-start.15
  182.8 6.2 collective-permute-start.16
  183.2 5.8 collective-permute-start.17
  280.7 5.6 collective-permute-start.19
  286.4 6.2 collective-permute-start.20
  286.4 6.2 collective-permute-start.21
  386.3 5.6 collective-permute-start.23
  392.0 6.2 collective-permute-start.24
  392.1 6.2 collective-permute-start.25
  404.7 6.4 collective-permute-start.28
  404.7 6.3 collective-permute-start.29
  411.2 8.6 %collective-permute-start.30 = (f32[64,1,130]{2,0,1:T(8,128)S(1)}, f32[64,1,130]{2,0,1:T(8,128)S(1)}, u32[]{:S(2)}, u32[]{:S(2)}) collective-permute-start(f32[64,1,130]{2,0,1:T(8,128)S(1)} %get-tuple-element.348), channel_id=1, source_target_pairs={{0,1},{1,2},{2,3},{3,0},{4,5},{5,6},{6,7},{7,4},{8,9},{9,10},{10,1... | collective-permute-start | bytes 99848 | tf_op jit(solution)/shard_map/ppermute | solution.py:17
  413.4 6.3 collective-permute-start.31
  464.2 5.6 collective-permute-start.33
  469.9 6.2 collective-permute-start.34
  471.5 6.1 collective-permute-start.35
  565.1 5.6 collective-permute-start.37
  570.8 6.2 collective-permute-start.38
  571.0 6.0 collective-permute-start.39
  674.4 6.2 collective-permute-start.42
  674.4 6.2 collective-permute-start.43
  779.8 6.2 collective-permute-start.46
  779.9 6.2 collective-permute-start.47
  (25 other events, 110.5 us)
where the time goes:
time: 791 us; the launch traced here: 787 us
  blocking collectives  566 us (72%)
  starting transfers between devices  82.8 us (10%)
  waiting for transfers between devices  61.1 us (8%)
  other arithmetic  33.4 us (4%)
  between operations  28 us (4%)
  local copies, waits for them, and re-layouts  15.5 us (2%)
    psum x8, blocking collectives, local(): lax.psum(jnp.stack([jnp.sum(image * image), jnp.sum(residual * image)]),...  330 us
    psum x6, blocking collectives, local(): lax.psum(jnp.stack([jnp.sum(image * images[member]) for member in range(i...  237 us
    ppermute x22, starting transfers between devices, extended(): lax.ppermute(lax.slice_in_dim(block, 0, width, axis=dim), axis, backward)  64.4 us
    ppermute x22, waiting for transfers between devices, extended(): lax.ppermute(lax.slice_in_dim(block, block.shape[dim] - width, None, axis...  53.3 us
  transfers between devices with their start and end apart: 48, of which 34 were waited for; matrix products, arithmetic and copies ran while one was open for 0% of the time, Pallas kernels for 0%

commit v1 on v0

v1 whole, which is shorter than its diff:
```python
import functools

import jax
import jax.numpy as jnp
from jax import lax
from jax.experimental import pallas as pl
from jax.experimental.pallas import tpu as pltpu
from jax.sharding import PartitionSpec as P

BLOCK = 4
ITERS = 4
OUTER = 2
SHIFT = 3.0
MESH = pl.DeviceIdType.MESH


def solve(gram, right):
    size = len(right)
    gram = [row[:] for row in gram]
    right = right[:]
    first = [gram[i][i] for i in range(size)]
    inverse = []
    for k in range(size):
        inverse.append(jnp.where(gram[k][k] > 1e-7 * first[k], 1.0 / gram[k][k], 0.0))
        for i in range(k + 1, size):
            factor = gram[k][i] * inverse[k]
            for j in range(i, size):
                gram[i][j] = gram[i][j] - factor * gram[k][j]
            right[i] = right[i] - factor * right[k]
    weights = [None] * size
    for k in reversed(range(size)):
        total = right[k]
        for j in range(k + 1, size):
            total = total - gram[k][j] * weights[j]
        weights[k] = total * inverse[k]
    return weights


def kernel(
    npx, npy, ny, nb, nx,
    vel_ref, pres_ref, mass_ref, face_ref, vert_ref, inv_ref, orient_ref,
    p_out, u_out,
    wide, mass, ce, cw, cn, cs, wu, wl, xc, binv, prs, fe, fn, fwx, fs, res,
    W, V, seam, hs, hn, hs0, pk, xw, xe, pk0, xw0, red,
    send_y, recv_y, send_x, recv_x, send_r, recv_r,
):
    levels = BLOCK * nb
    tiles = levels // 8
    count = npx * npy
    px, py = lax.axis_index("px"), lax.axis_index("py")
    east, west = lax.rem(px + 1, npx), lax.rem(px + npx - 1, npx)
    has_north, has_south = py < npy - 1, py > 0
    me = px * npy + py

    barrier = pltpu.get_barrier_semaphore()

    def partner(step):
        other = lax.rem(me + step, count)
        return (lax.div(other, npy), lax.rem(other, npy))

    def greet(step, carry):
        pl.semaphore_signal(barrier, inc=1, device_id=partner(step), device_id_type=MESH)
        return carry

    lax.fori_loop(1, count, greet, 0)

    def gather(ref, base, y):
        return jnp.concatenate(
            [
                ref[pl.ds(base + m * ny + y, nb, stride=BLOCK * ny), :]
                for m in range(BLOCK)
            ],
            axis=0,
        )

    def scatter(ref, base, y, value):
        for m in range(BLOCK):
            ref[pl.ds(base + m * ny + y, nb, stride=BLOCK * ny), :] = value[m * nb : (m + 1) * nb]

    lane = lax.broadcasted_iota(jnp.int32, (8, nx), 1)
    lane_l = lax.broadcasted_iota(jnp.int32, (levels, nx), 1)
    even = lax.rem(lane, 2) == 0

    def pack(slabs):
        total = jnp.zeros((8, nx), jnp.float32)
        for y in range(ny):
            for t in range(tiles):
                i = y * tiles + t
                turned = slabs[y][t * 8 : (t + 1) * 8]
                if i:
                    turned = pltpu.roll(turned, 2 * i, axis=1)
                mine = (lane == 2 * i) | (lane == (2 * i - 1) % nx)
                total = jnp.where(mine, turned, total)
        return total

    def meet(from_west, from_east):
        return jnp.where(even, pltpu.roll(from_west, 1, axis=1), pltpu.roll(from_east, nx - 1, axis=1))

    def spread(packed, y):
        parts = []
        for t in range(tiles):
            i = y * tiles + t
            parts.append(pltpu.roll(packed, nx - 2 * i, axis=1) if i else packed)
        return jnp.concatenate(parts, axis=0)

    def up(slab):
        return jnp.concatenate([slab[nb:], pltpu.roll(slab[:nb], nb - 1, axis=0)], axis=0)

    def down(slab):
        return jnp.concatenate([pltpu.roll(slab[levels - nb :], 1, axis=0), slab[: levels - nb]], axis=0)

    def roll_w(slab):
        return pltpu.roll(slab, 1, axis=1)

    def roll_e(slab):
        return pltpu.roll(slab, nx - 1, axis=1)

    def y_copies(low, high, low_dst, high_dst, k):
        north = pltpu.make_async_remote_copy(
            src_ref=high, dst_ref=high_dst, send_sem=send_y.at[k, 0], recv_sem=recv_y.at[k, 0],
            device_id=(px, py + 1), device_id_type=MESH)
        south = pltpu.make_async_remote_copy(
            src_ref=low, dst_ref=low_dst, send_sem=send_y.at[k, 1], recv_sem=recv_y.at[k, 1],
            device_id=(px, py - 1), device_id_type=MESH)
        return north, south

    def x_copies(to_east, to_west, east_dst, west_dst, k):
        a = pltpu.make_async_remote_copy(
            src_ref=to_east, dst_ref=east_dst, send_sem=send_x.at[k, 0], recv_sem=recv_x.at[k, 0],
            device_id=(east, py), device_id_type=MESH)
        b = pltpu.make_async_remote_copy(
            src_ref=to_west, dst_ref=west_dst, send_sem=send_x.at[k, 1], recv_sem=recv_x.at[k, 1],
            device_id=(west, py), device_id_type=MESH)
        return a, b

    def start(copies):
        (north, south), (a, b) = copies

        @pl.when(has_north)
        def _():
            north.start()

        @pl.when(has_south)
        def _():
            south.start()

        a.start()
        b.start()

    def finish(copies):
        (north, south), (a, b) = copies
        a.wait_recv()
        b.wait_recv()

        @pl.when(has_south)
        def _():
            north.wait_recv()

        @pl.when(has_north)
        def _():
            south.wait_recv()

    def sent(copies):
        (north, south), (a, b) = copies
        a.wait_send()
        b.wait_send()

        @pl.when(has_north)
        def _():
            north.wait_send()

        @pl.when(has_south)
        def _():
            south.wait_send()

    wide[0] = face_ref[0 : levels * ny].astype(jnp.float32)
    wide[1] = face_ref[levels * ny :].astype(jnp.float32)
    sign = 2.0 * orient_ref[...].astype(jnp.float32) - 1.0
    for y in range(ny):
        ce[y] = gather(wide.at[0], 0, y)
        cn[y] = gather(wide.at[1], 0, y)
        prs[y] = gather(pres_ref, 0, y)
        fe[y] = sign[y : y + 1] * gather(vel_ref, 0, y)
        fn[y] = sign[ny + y : ny + y + 1] * gather(vel_ref, levels * ny, y)
    seam[0] = prs[ny - 1]
    seam[1] = fn[ny - 1]
    seam[2] = cn[ny - 1]
    pk0[0] = pack(prs)
    pk0[1] = pack(fe)
    pk0[2] = pack(ce)

    @pl.when(jnp.logical_not(has_south))
    def _():
        hs0[...] = jnp.zeros_like(hs0)
        hs[...] = jnp.zeros_like(hs)

    @pl.when(jnp.logical_not(has_north))
    def _():
        hn[...] = jnp.zeros_like(hn)

    pl.semaphore_wait(barrier, count - 1)

    first = (
        y_copies(prs.at[0], seam, hn.at[0], hs0, 0),
        x_copies(pk0, pk0.at[0], xw0, xe.at[0], 0),
    )
    start(first)

    wide[0] = mass_ref[...].astype(jnp.float32)
    wide[1] = jnp.zeros_like(wide[1])
    wide[1, 0 : (levels - 1) * ny, :] = vert_ref[...].astype(jnp.float32)
    for j in range(BLOCK):
        wide[2 + j] = inv_ref[j * levels * ny : (j + 1) * levels * ny].astype(jnp.float32)
    for y in range(ny):
        mass[y] = gather(wide.at[0], 0, y)
        slab = gather(wide.at[1], 0, y)
        wu[y] = slab
        wl[y] = down(slab)
        for j in range(BLOCK):
            binv[j, y] = gather(wide.at[2 + j], 0, y)

    finish(first)
    sent(first)
    packed_c = meet(xw0[2], xw0[2])
    packed_f = meet(xw0[1], xw0[1])
    for y in range(ny):
        left = jnp.where(lane_l == 0, spread(packed_c, y), roll_w(ce[y]))
        cw[y] = left
        cs[y] = hs0[2] if y == 0 else cn[y - 1]
        xc[y] = jnp.where(lane_l == 0, left, jnp.where(lane_l == nx - 1, ce[y], 0.0))
        fwx[y] = spread(packed_f, y)
    fs[...] = hs0[1]

    def inside(values, y):
        v = values[y]
        to_east = jnp.where(lane_l == nx - 1, 0.0, roll_e(v))
        to_west = jnp.where(lane_l == 0, 0.0, roll_w(v))
        total = mass[y] * v + ce[y] * (v - to_east) + cw[y] * (v - to_west)
        total += cn[y] * (v - values[y + 1]) if y < ny - 1 else cn[y] * v
        total += cs[y] * (v - values[y - 1]) if y > 0 else cs[y] * v
        return total + wu[y] * (v - up(v)) + wl[y] * (v - down(v))

    def rim(y, packed, south, north):
        total = xc[y] * spread(packed, y)
        if y == 0:
            total += cs[y] * south
        if y == ny - 1:
            total += cn[y] * north
        return total

    def precondition(blocks, y):
        parts = []
        for m in range(BLOCK):
            rows = slice(m * nb, (m + 1) * nb)
            total = binv[0, y, rows] * blocks[0:nb]
            for j in range(1, BLOCK):
                total += binv[j, y, rows] * blocks[j * nb : (j + 1) * nb]
            parts.append(total)
        return jnp.concatenate(parts, axis=0)

    def fold(slab):
        total = slab[0:8]
        for t in range(1, tiles):
            total += slab[t * 8 : (t + 1) * 8]
        return total

    p_south, p_north = hs0[0], hn[0]
    p_packed = meet(xw0[0], xe[0])

    for outer in range(OUTER):
        for y in range(ny):
            f_west = jnp.where(lane_l == 0, fwx[y], roll_w(fe[y]))
            f_south = fs[...] if y == 0 else fn[y - 1]
            div = fe[y] - f_west + fn[y] - f_south
            image = inside(prs, y) - rim(y, p_packed, p_south, p_north)
            residual = mass[y] * prs[y] - div - image
            res[y] = residual
            W[0, y] = precondition(residual, y)
        packs = []
        souths, norths = [], []
        dots = {}
        for i in range(ITERS):
            k = 1 + outer * ITERS + i
            pk[k - 1] = pack([W[i, y] for y in range(ny)])
            for_y = y_copies(W.at[i, 0], W.at[i, ny - 1], hn.at[k], hs.at[k - 1], k)
            copies = (for_y, x_copies(pk.at[k - 1], pk.at[k - 1], xw.at[k - 1], xe.at[k], k))
            start(copies)
            for y in range(ny):
                V[i, y] = inside(W.at[i], y)
            if i > 0:
                for j in range(i):
                    dots[j, i - 1] = sum(fold(V[j, y] * V[i - 1, y]) for y in range(ny))
                dots["r", i - 1] = sum(fold(res[y] * V[i - 1, y]) for y in range(ny))
            finish(copies)
            packed = meet(xw[k - 1], xe[k])
            packs.append(packed)
            for y in range(ny):
                image = V[i, y] - rim(y, packed, hs[k - 1], hn[k])
                V[i, y] = image
                if i < ITERS - 1:
                    W[i + 1, y] = precondition(image, y) - SHIFT * W[i, y]
            sent(copies)
        last = ITERS - 1
        for j in range(ITERS):
            dots[j, last] = sum(fold(V[j, y] * V[last, y]) for y in range(ny))
        dots["r", last] = sum(fold(res[y] * V[last, y]) for y in range(ny))

        order = [(j, i) for i in range(ITERS) for j in range(i + 1)]
        order += [("r", i) for i in range(ITERS)]
        rows = [jnp.sum(dots[key], axis=0, keepdims=True) for key in order]
        rows += [jnp.zeros_like(rows[0])] * (16 - len(rows))
        low, high = jnp.concatenate(rows[:8], axis=0), jnp.concatenate(rows[8:], axis=0)
        half = nx // 2
        low += pltpu.roll(low, half, axis=1)
        high += pltpu.roll(high, half, axis=1)
        red[outer, me] = jnp.where(lane < half, low, high)

        def share(step, carry):
            pltpu.make_async_remote_copy(
                src_ref=red.at[outer, me], dst_ref=red.at[outer, me],
                send_sem=send_r.at[outer], recv_sem=recv_r.at[outer],
                device_id=partner(step), device_id_type=MESH).start()
            return carry

        lax.fori_loop(1, count, share, 0)
        rest = red.at[outer, pl.ds(0, count - 1)]
        pltpu.make_async_copy(rest, rest, recv_r.at[outer]).wait()
        pltpu.make_async_copy(rest, rest, send_r.at[outer]).wait()
        total = jnp.sum(red[outer], axis=0)
        low = jnp.sum(jnp.where(lane < half, total, 0.0), axis=1, keepdims=True)
        high = jnp.sum(jnp.where(lane < half, 0.0, total), axis=1, keepdims=True)
        sums = {}
        for n, key in enumerate(order):
            column = low if n < 8 else high
            sums[key] = jnp.broadcast_to(column[n % 8 : n % 8 + 1], (8, nx))
        gram = [[sums[min(i, j), max(i, j)] for j in range(ITERS)] for i in range(ITERS)]
        weights = solve(gram, [sums["r", i] for i in range(ITERS)])
        wide_weights = [jnp.broadcast_to(c[0:1], (levels, nx)) for c in weights]

        for i in range(ITERS):
            k = 1 + outer * ITERS + i
            p_packed += weights[i] * packs[i]
            p_south += wide_weights[i] * hs[k - 1]
            p_north += wide_weights[i] * hn[k]
        for y in range(ny):
            value = prs[y]
            for i in range(ITERS):
                value += wide_weights[i] * W[i, y]
            prs[y] = value
        for y in range(ny):
            value = prs[y]
            edge = spread(p_packed, y)
            to_east = jnp.where(lane_l == nx - 1, edge, roll_e(value))
            to_north = prs[y + 1] if y < ny - 1 else p_north
            fe[y] = fe[y] + ce[y] * (value - to_east)
            fn[y] = fn[y] + cn[y] * (value - to_north)
            if outer < OUTER - 1:
                fwx[y] = fwx[y] + cw[y] * (edge - value)
                if y == 0:
                    fs[...] = fs[...] + cs[0] * (p_south - value)
            else:
                scatter(p_out, 0, y, value)
                scatter(u_out, 0, y, sign[y : y + 1] * fe[y])
                scatter(u_out, levels * ny, y, sign[ny + y : ny + y + 1] * fn[y])


def local(npx, npy, velocity, pressure, mass, face_coeff, vert_coeff, block_inverse, orientation):
    levels, ny, nx = pressure.shape
    nb = levels // BLOCK
    f32 = jnp.float32
    rounds = OUTER * ITERS
    field = pltpu.VMEM((ny, levels, nx), f32)
    slab = pltpu.VMEM((levels, nx), f32)
    inputs = [a.reshape(-1, nx) for a in (velocity, pressure, mass, face_coeff, vert_coeff, block_inverse, orientation)]
    vmem = pl.BlockSpec(memory_space=pltpu.VMEM)
    scratch = dict(
        wide=pltpu.VMEM((2 + BLOCK, levels * ny, nx), f32),
        mass=field, ce=field, cw=field, cn=field, cs=field, wu=field, wl=field, xc=field,
        binv=pltpu.VMEM((BLOCK, ny, levels, nx), f32),
        prs=field, fe=field, fn=field, fwx=field, fs=slab, res=field,
        W=pltpu.VMEM((ITERS, ny, levels, nx), f32),
        V=pltpu.VMEM((ITERS, ny, levels, nx), f32),
        seam=pltpu.VMEM((3, levels, nx), f32),
        hs=pltpu.VMEM((rounds, levels, nx), f32),
        hn=pltpu.VMEM((rounds + 1, levels, nx), f32),
        hs0=pltpu.VMEM((3, levels, nx), f32),
        pk=pltpu.VMEM((rounds, 8, nx), f32),
        xw=pltpu.VMEM((rounds, 8, nx), f32),
        xe=pltpu.VMEM((rounds + 1, 8, nx), f32),
        pk0=pltpu.VMEM((3, 8, nx), f32),
        xw0=pltpu.VMEM((3, 8, nx), f32),
        red=pltpu.VMEM((OUTER, npx * npy, 8, nx), f32),
        send_y=pltpu.SemaphoreType.DMA((rounds + 1, 2)),
        recv_y=pltpu.SemaphoreType.DMA((rounds + 1, 2)),
        send_x=pltpu.SemaphoreType.DMA((rounds + 1, 2)),
        recv_x=pltpu.SemaphoreType.DMA((rounds + 1, 2)),
        send_r=pltpu.SemaphoreType.DMA((OUTER,)),
        recv_r=pltpu.SemaphoreType.DMA((OUTER,)),
    )
    p_new, u_new = pl.pallas_call(
        functools.partial(kernel, npx, npy, ny, nb, nx),
        out_shape=(
            jax.ShapeDtypeStruct((levels * ny, nx), f32),
            jax.ShapeDtypeStruct((2 * levels * ny, nx), f32),
        ),
        in_specs=[vmem] * 7,
        out_specs=(vmem, vmem),
        scratch_shapes=list(scratch.values()),
        compiler_params=pltpu.CompilerParams(
            collective_id=0, has_side_effects=True, vmem_limit_bytes=40 * 1024 * 1024
        ),
    )(*inputs)
    return p_new.reshape(pressure.shape), u_new.reshape(velocity.shape)


def solution(mesh):
    placed = (
        P(None, None, "py", "px"),
        P(None, "py", "px"),
        P(None, "py", "px"),
        P(None, None, "py", "px"),
        P(None, "py", "px"),
        P(None, None, "py", "px"),
        P(None, "py", "px"),
    )
    return jax.shard_map(
        functools.partial(local, mesh.shape["px"], mesh.shape["py"]),
        mesh=mesh,
        in_specs=placed,
        out_specs=(P(None, "py", "px"), P(None, None, "py", "px")),
        check_vma=False,
    )
```

time: 791 us -> 55.9 us (0.07)
  blocking collectives: 566 us -> 0 us
  starting transfers between devices: 82.8 us -> 0 us
  waiting for transfers between devices: 61.1 us -> 0 us
  Pallas kernels: 0 us -> 49.1 us
  other arithmetic: 33.4 us -> 0 us
  between operations: 28 us -> 0.68 us
  local copies, waits for them, and re-layouts: 15.5 us -> 5.92 us
    psum x14 -> x0, blocking collectives: 566 us -> none  [the longest x8 330 us: local(): lax.psum(jnp.stack([jnp.sum(image * image), jnp.sum(residual * image)]),...]
    ppermute x48 -> x0, starting transfers between devices: 82.8 us -> none  [the longest x22 64.4 us: extended(): lax.ppermute(lax.slice_in_dim(block, 0, width, axis=dim), axis, backward)]
    ppermute x48 -> x0, waiting for transfers between devices: 61.1 us -> none  [the longest x22 53.3 us: extended(): lax.ppermute(lax.slice_in_dim(block, block.shape[dim] - width, None, axis...]
    pallas_call x0 -> x1, Pallas kernels: none -> 49.1 us  [local(): pl.pallas_call(functools.partial(kernel, npx, npy, ny, nb, nx), out_shape...]
    another operation x42 -> x0, other arithmetic: 17.7 us -> none  [the longest x8 10.7 us: local(): jnp.stack([jnp.sum(image * image), jnp.sum(residual * image)])]
    reduce_sum x14 -> x0, other arithmetic: 11.1 us -> none  [the longest x8 5.91 us: local(): jnp.sum(image * image)]
    slice x50 -> x0, local copies, waits for them, and re-layouts: 10.9 us -> none  [the longest x8 4.77 us: local(): image_norm = pair_sums[0]]
  transfers between devices with their start and end apart: 48 -> 0, of which waited for: 34 -> 0; matrix products, arithmetic and copies ran while one was open for 0% -> 0% of each run, Pallas kernels for 0% -> 0%
where the time goes in v1:
time: 55.9 us; the launch traced here: 55.7 us
  Pallas kernels  49.1 us (88%)
  local copies, waits for them, and re-layouts  5.92 us (11%)
  between operations  0.68 us (1%)
    pallas_call x1, Pallas kernels, local(): pl.pallas_call(functools.partial(kernel, npx, npy, ny, nb, nx), out_shape...  49.1 us
    unnamed x14, local copies, waits for them, and re-layouts  5.01 us

profile of v1, /device:TPU:0, one launch (start us, length us, event | category | flops | bytes accessed | tf_op | source)
XLA Modules:
  0.0 55.7 jit_solution(11267856764167708561)
XLA Ops:
  0.6 0.0 copy-start.2
  0.6 0.0 copy-start.5
  0.7 0.9 %reshape.35.vert_ref = bf16[252,128]{1,0:T(8,128)(2,1)S(1)} reshape(bf16[63,4,128]{2,1,0:T(4,128)(2,1)} %param.11) | data formatting | bytes 129024 | tf_op jit(solution)/shard_map/reshape | solution.py:374
  1.6 0.0 copy-done.2
  1.6 0.0 copy-done.5
  1.6 0.0 copy-start
  1.6 0.9 %copy-done = f32[2,64,4,128]{3,2,1,0:T(4,128)S(1)} copy-done((f32[2,64,4,128]{3,2,1,0:T(4,128)S(1)}, f32[2,64,4,128]{3,2,1,0:T(4,128)}, u32[]{:S(2)}) %copy-start) | copy-done | bytes 262168
  2.5 0.0 copy-start.1
  2.5 0.9 %copy-done.1 = bf16[4,64,4,128]{3,2,1,0:T(4,128)(2,1)S(1)} copy-done((bf16[4,64,4,128]{3,2,1,0:T(4,128)(2,1)S(1)}, bf16[4,64,4,128]{3,2,1,0:T(4,128)(2,1)}, u32[]{:S(2)}) %copy-start.1) | copy-done | bytes 262168
  3.5 0.0 copy-start.3
  3.5 0.9 %copy-done.3 = bf16[2,64,4,128]{3,2,1,0:T(4,128)(2,1)S(1)} copy-done((bf16[2,64,4,128]{3,2,1,0:T(4,128)(2,1)S(1)}, bf16[2,64,4,128]{3,2,1,0:T(4,128)(2,1)}, u32[]{:S(2)}) %copy-start.3) | copy-done | bytes 131096
  4.4 0.0 copy-start.4
  4.4 0.8 %copy-done.4 = bf16[64,4,128]{2,1,0:T(4,128)(2,1)S(1)} copy-done((bf16[64,4,128]{2,1,0:T(4,128)(2,1)S(1)}, bf16[64,4,128]{2,1,0:T(4,128)(2,1)}, u32[]{:S(2)}) %copy-start.4) | copy-done | bytes 65560
  5.2 49.1 %shard_map.86 = (f32[256,128]{1,0:T(8,128)S(1)}, f32[512,128]{1,0:T(8,128)S(1)}) custom-call(f32[512,128]{1,0:T(8,128)S(1)} %bitcast.8, f32[256,128]{1,0:T(8,128)S(1)} %bitcast.11, bf16[256,128]{1,0:T(8,128)(2,1)S(1)} %bitcast.14, bf16[512,128]{1,0:T(8,128)(2,1)S(1)} %bitcast.12, bf16[252,128]{1,0:T(8,128)(2,1)S(1)} %reshape.35.vert_ref, ...), custom_call_target="tpu_custom_call" | custom-call | tf_op jit(solution)/shard_map/pallas_call | solution.py:400
  54.3 0.7 %copy.11 = f32[64,4,128]{2,1,0:T(4,128)} copy(f32[64,4,128]{2,1,0:T(4,128)S(1)} %bitcast.13) | data formatting | bytes 262144
  55.0 0.7 %copy.12 = f32[2,64,4,128]{3,2,1,0:T(4,128)} copy(f32[2,64,4,128]{3,2,1,0:T(4,128)S(1)} %bitcast.10) | data formatting | bytes 524288
Async XLA Ops:
  0.6 0.9 %copy-start.2 = (f32[64,4,128]{2,1,0:T(4,128)S(1)}, f32[64,4,128]{2,1,0:T(4,128)}, u32[]{:S(2)}) copy-start(f32[64,4,128]{2,1,0:T(4,128)} %param.8) | copy-start | bytes 393220
  0.6 0.9 %copy-start.5 = (s32[2,4,128]{2,1,0:T(4,128)S(1)}, s32[2,4,128]{2,1,0:T(4,128)}, u32[]{:S(2)}) copy-start(s32[2,4,128]{2,1,0:T(4,128)} %param.13) | copy-start | bytes 12292
  1.6 1.0 %copy-start = (f32[2,64,4,128]{3,2,1,0:T(4,128)S(1)}, f32[2,64,4,128]{3,2,1,0:T(4,128)}, u32[]{:S(2)}) copy-start(f32[2,64,4,128]{3,2,1,0:T(4,128)} %param.7) | copy-start | bytes 786436
  2.5 0.9 %copy-start.1 = (bf16[4,64,4,128]{3,2,1,0:T(4,128)(2,1)S(1)}, bf16[4,64,4,128]{3,2,1,0:T(4,128)(2,1)}, u32[]{:S(2)}) copy-start(bf16[4,64,4,128]{3,2,1,0:T(4,128)(2,1)} %param.12) | copy-start | bytes 786436
  3.5 0.9 %copy-start.3 = (bf16[2,64,4,128]{3,2,1,0:T(4,128)(2,1)S(1)}, bf16[2,64,4,128]{3,2,1,0:T(4,128)(2,1)}, u32[]{:S(2)}) copy-start(bf16[2,64,4,128]{3,2,1,0:T(4,128)(2,1)} %param.10) | copy-start | bytes 393220
  4.4 0.8 %copy-start.4 = (bf16[64,4,128]{2,1,0:T(4,128)(2,1)S(1)}, bf16[64,4,128]{2,1,0:T(4,128)(2,1)}, u32[]{:S(2)}) copy-start(bf16[64,4,128]{2,1,0:T(4,128)(2,1)} %param.9) | copy-start | bytes 196612

commit v2 on v1

--- a/solution.py
+++ b/solution.py
@@ -38,11 +38,12 @@
 
 def kernel(
     npx, npy, ny, nb, nx,
+    vel_hbm, pres_hbm, mass_hbm, face_hbm, vert_hbm, inv_hbm, orient_hbm,
+    p_out, u_out,
     vel_ref, pres_ref, mass_ref, face_ref, vert_ref, inv_ref, orient_ref,
-    p_out, u_out,
-    wide, mass, ce, cw, cn, cs, wu, wl, xc, binv, prs, fe, fn, fwx, fs, res,
-    W, V, seam, hs, hn, hs0, pk, xw, xe, pk0, xw0, red,
-    send_y, recv_y, send_x, recv_x, send_r, recv_r,
+    wide, wide_w, mass, ce, cw, cn, cs, wu, wl, xc, binv, prs, fe, fn, res, G, MG, gs, gn, gpk, gxw, gxe,
+    W, V, low_p, seam, hs, hn, hs0, pk, xw, xe, pk0, xw0, red,
+    send_y, recv_y, send_x, recv_x, send_r, recv_r, fetch,
 ):
     levels = BLOCK * nb
     tiles = levels // 8
@@ -54,15 +55,22 @@
 
     barrier = pltpu.get_barrier_semaphore()
 
-    def partner(step):
-        other = lax.rem(me + step, count)
-        return (lax.div(other, npy), lax.rem(other, npy))
-
-    def greet(step, carry):
-        pl.semaphore_signal(barrier, inc=1, device_id=partner(step), device_id_type=MESH)
-        return carry
-
-    lax.fori_loop(1, count, greet, 0)
+    partners = [
+        (lax.rem(px + i, npx), lax.rem(py + j, npy))
+        for i in range(npx) for j in range(npy) if i or j
+    ]
+    for target in partners:
+        pl.semaphore_signal(barrier, inc=1, device_id=target, device_id_type=MESH)
+
+    fetches = [
+        pltpu.make_async_copy(src, dst, fetch.at[n])
+        for n, (src, dst) in enumerate([
+            (face_hbm, face_ref), (pres_hbm, pres_ref), (vel_hbm, vel_ref), (orient_hbm, orient_ref),
+            (mass_hbm, mass_ref), (vert_hbm, vert_ref), (inv_hbm, inv_ref),
+        ])
+    ]
+    for copy in fetches:
+        copy.start()
 
     def gather(ref, base, y):
         return jnp.concatenate(
@@ -80,6 +88,8 @@
     lane = lax.broadcasted_iota(jnp.int32, (8, nx), 1)
     lane_l = lax.broadcasted_iota(jnp.int32, (levels, nx), 1)
     even = lax.rem(lane, 2) == 0
+    lane_16 = lax.broadcasted_iota(jnp.int32, (16, nx), 1)
+    group = lax.broadcasted_iota(jnp.int32, (16, nx), 0)
 
     def pack(slabs):
         total = jnp.zeros((8, nx), jnp.float32)
@@ -173,6 +183,8 @@
         def _():
             south.wait_send()
 
+    for copy in fetches[:4]:
+        copy.wait()
     wide[0] = face_ref[0 : levels * ny].astype(jnp.float32)
     wide[1] = face_ref[levels * ny :].astype(jnp.float32)
     sign = 2.0 * orient_ref[...].astype(jnp.float32) - 1.0
@@ -183,6 +195,7 @@
         fe[y] = sign[y : y + 1] * gather(vel_ref, 0, y)
         fn[y] = sign[ny + y : ny + y + 1] * gather(vel_ref, levels * ny, y)
     seam[0] = prs[ny - 1]
+    low_p[...] = prs[0]
     seam[1] = fn[ny - 1]
     seam[2] = cn[ny - 1]
     pk0[0] = pack(prs)
@@ -193,34 +206,39 @@
     def _():
         hs0[...] = jnp.zeros_like(hs0)
         hs[...] = jnp.zeros_like(hs)
+        gs[...] = jnp.zeros_like(gs)
 
     @pl.when(jnp.logical_not(has_north))
     def _():
         hn[...] = jnp.zeros_like(hn)
+        gn[...] = jnp.zeros_like(gn)
 
     pl.semaphore_wait(barrier, count - 1)
 
     first = (
-        y_copies(prs.at[0], seam, hn.at[0], hs0, 0),
+        y_copies(low_p, seam, hn.at[0], hs0, 0),
         x_copies(pk0, pk0.at[0], xw0, xe.at[0], 0),
     )
     start(first)
 
+    for copy in fetches[4:]:
+        copy.wait()
     wide[0] = mass_ref[...].astype(jnp.float32)
-    wide[1] = jnp.zeros_like(wide[1])
-    wide[1, 0 : (levels - 1) * ny, :] = vert_ref[...].astype(jnp.float32)
+    wide_w[0 : levels - 1] = vert_ref[...].astype(jnp.float32)
+    wide_w[levels - 1] = jnp.zeros((ny, nx), jnp.float32)
     for j in range(BLOCK):
-        wide[2 + j] = inv_ref[j * levels * ny : (j + 1) * levels * ny].astype(jnp.float32)
+        wide[1 + j] = inv_ref[j * levels * ny : (j + 1) * levels * ny].astype(jnp.float32)
     for y in range(ny):
         mass[y] = gather(wide.at[0], 0, y)
-        slab = gather(wide.at[1], 0, y)
+        slab = jnp.concatenate(
+            [wide_w[pl.ds(m, nb, stride=BLOCK), y, :] for m in range(BLOCK)], axis=0
+        )
         wu[y] = slab
         wl[y] = down(slab)
         for j in range(BLOCK):
-            binv[j, y] = gather(wide.at[2 + j], 0, y)
+            binv[j, y] = gather(wide.at[1 + j], 0, y)
 
     finish(first)
-    sent(first)
     packed_c = meet(xw0[2], xw0[2])
     packed_f = meet(xw0[1], xw0[1])
     for y in range(ny):
@@ -228,17 +246,15 @@
         cw[y] = left
         cs[y] = hs0[2] if y == 0 else cn[y - 1]
         xc[y] = jnp.where(lane_l == 0, left, jnp.where(lane_l == nx - 1, ce[y], 0.0))
-        fwx[y] = spread(packed_f, y)
-    fs[...] = hs0[1]
 
     def inside(values, y):
         v = values[y]
         to_east = jnp.where(lane_l == nx - 1, 0.0, roll_e(v))
         to_west = jnp.where(lane_l == 0, 0.0, roll_w(v))
-        total = mass[y] * v + ce[y] * (v - to_east) + cw[y] * (v - to_west)
-        total += cn[y] * (v - values[y + 1]) if y < ny - 1 else cn[y] * v
-        total += cs[y] * (v - values[y - 1]) if y > 0 else cs[y] * v
-        return total + wu[y] * (v - up(v)) + wl[y] * (v - down(v))
+        flat = ce[y] * (v - to_east) + cw[y] * (v - to_west)
+        flat += cn[y] * (v - values[y + 1]) if y < ny - 1 else cn[y] * v
+        flat += cs[y] * (v - values[y - 1]) if y > 0 else cs[y] * v
+        return flat, mass[y] * v + flat + wu[y] * (v - up(v)) + wl[y] * (v - down(v))
 
     def rim(y, packed, south, north):
         total = xc[y] * spread(packed, y)
@@ -267,39 +283,100 @@
     p_south, p_north = hs0[0], hn[0]
     p_packed = meet(xw0[0], xe[0])
 
+    pending = []
+
+    def offer(n):
+        gpk[n] = pack([MG[n, y] for y in range(ny)])
+        k = 1 + OUTER * ITERS + n
+        copies = (
+            y_copies(MG.at[n, 0], MG.at[n, ny - 1], gn.at[n], gs.at[n], k),
+            x_copies(gpk.at[n], gpk.at[n], gxw.at[n], gxe.at[n], k),
+        )
+        start(copies)
+        pending.append(copies)
+        return copies
+
+    def combine(first, terms, factors):
+        for term, factor in zip(terms, factors):
+            first += factor * term
+        return first
+
+    for y in range(ny):
+        f_west = jnp.where(lane_l == 0, spread(packed_f, y), roll_w(fe[y]))
+        f_south = hs0[1] if y == 0 else fn[y - 1]
+        div = fe[y] - f_west + fn[y] - f_south
+        flat, image = inside(prs, y)
+        border = rim(y, p_packed, p_south, p_north)
+        residual = mass[y] * prs[y] - div - (image - border)
+        res[y] = residual
+        W[0, y] = precondition(residual, y)
+        G[ITERS, y] = residual - (flat - border)
+
+    def update(outer, packs, souths, norths, weights, wide_weights, state):
+        p_packed, p_south, p_north = state
+        p_packed = combine(p_packed, packs, weights)
+        p_south = combine(p_south, souths, wide_weights)
+        p_north = combine(p_north, norths, wide_weights)
+        for y in range(ny):
+            prs[y] = combine(prs[y], [W[outer * ITERS + i, y] for i in range(ITERS)], wide_weights)
+        for y in range(ny):
+            value = prs[y]
+            to_east = jnp.where(lane_l == nx - 1, spread(p_packed, y), roll_e(value))
+            to_north = prs[y + 1] if y < ny - 1 else p_north
+            fe[y] = fe[y] + ce[y] * (value - to_east)
+            fn[y] = fn[y] + cn[y] * (value - to_north)
+        return p_packed, p_south, p_north
+
+    state = (p_packed, p_south, p_north)
+    late = None
+    offers = []
     for outer in range(OUTER):
-        for y in range(ny):
-            f_west = jnp.where(lane_l == 0, fwx[y], roll_w(fe[y]))
-            f_south = fs[...] if y == 0 else fn[y - 1]
-            div = fe[y] - f_west + fn[y] - f_south
-            image = inside(prs, y) - rim(y, p_packed, p_south, p_north)
-            residual = mass[y] * prs[y] - div - image
-            res[y] = residual
-            W[0, y] = precondition(residual, y)
-        packs = []
-        souths, norths = [], []
+        start_w = outer * ITERS
+        packs, souths, norths = [], [], []
         dots = {}
         for i in range(ITERS):
             k = 1 + outer * ITERS + i
-            pk[k - 1] = pack([W[i, y] for y in range(ny)])
-            for_y = y_copies(W.at[i, 0], W.at[i, ny - 1], hn.at[k], hs.at[k - 1], k)
-            copies = (for_y, x_copies(pk.at[k - 1], pk.at[k - 1], xw.at[k - 1], xe.at[k], k))
-            start(copies)
+            ready = outer > 0 and i == 0
+            if not ready:
+                pk[k - 1] = pack([W[start_w + i, y] for y in range(ny)])
+                copies = (
+                    y_copies(W.at[start_w + i, 0], W.at[start_w + i, ny - 1], hn.at[k], hs.at[k - 1], k),
+                    x_copies(pk.at[k - 1], pk.at[k - 1], xw.at[k - 1], xe.at[k], k),
+                )
+                start(copies)
+                pending.append(copies)
             for y in range(ny):
-                V[i, y] = inside(W.at[i], y)
+                flat, image = inside(W.at[start_w + i], y)
+                V[i, y] = image
+                if outer < OUTER - 1:
+                    G[i, y] = mass[y] * W[start_w + i, y] - flat - image
             if i > 0:
                 for j in range(i):
                     dots[j, i - 1] = sum(fold(V[j, y] * V[i - 1, y]) for y in range(ny))
                 dots["r", i - 1] = sum(fold(res[y] * V[i - 1, y]) for y in range(ny))
-            finish(copies)
-            packed = meet(xw[k - 1], xe[k])
+            if outer < OUTER - 1:
+                term = (i - 1) % (ITERS + 1)
+                for y in range(ny):
+                    MG[term, y] = precondition(G[term, y], y)
+                offers.append((term, offer(term)))
+            if outer > 0 and i == 1:
+                state = update(outer - 1, *late, state)
+            if ready:
+                packed, south, north = started
+            else:
+                finish(copies)
+                packed, south, north = meet(xw[k - 1], xe[k]), hs[k - 1], hn[k]
             packs.append(packed)
+            souths.append(south)
+            norths.append(north)
             for y in range(ny):
-                image = V[i, y] - rim(y, packed, hs[k - 1], hn[k])
+                border = rim(y, packed, south, north)
+                image = V[i, y] - border
                 V[i, y] = image
                 if i < ITERS - 1:
-                    W[i + 1, y] = precondition(image, y) - SHIFT * W[i, y]
-            sent(copies)
+                    W[start_w + i + 1, y] = precondition(image, y) - SHIFT * W[start_w + i, y]
+                if outer < OUTER - 1:
+                    G[i, y] = G[i, y] + 2.0 * border
         last = ITERS - 1
         for j in range(ITERS):
             dots[j, last] = sum(fold(V[j, y] * V[last, y]) for y in range(ny))
@@ -309,59 +386,53 @@
         order += [("r", i) for i in range(ITERS)]
         rows = [jnp.sum(dots[key], axis=0, keepdims=True) for key in order]
         rows += [jnp.zeros_like(rows[0])] * (16 - len(rows))
-        low, high = jnp.concatenate(rows[:8], axis=0), jnp.concatenate(rows[8:], axis=0)
-        half = nx // 2
-        low += pltpu.roll(low, half, axis=1)
-        high += pltpu.roll(high, half, axis=1)
-        red[outer, me] = jnp.where(lane < half, low, high)
-
-        def share(step, carry):
+        rows = jnp.sum(jnp.concatenate(rows, axis=0), axis=1, keepdims=True)
+        red[outer, me] = jnp.sum(jnp.where(group == lane_16, rows, 0.0), axis=0, keepdims=True)
+        for target in partners:
             pltpu.make_async_remote_copy(
                 src_ref=red.at[outer, me], dst_ref=red.at[outer, me],
                 send_sem=send_r.at[outer], recv_sem=recv_r.at[outer],
-                device_id=partner(step), device_id_type=MESH).start()
-            return carry
-
-        lax.fori_loop(1, count, share, 0)
+                device_id=target, device_id_type=MESH).start()
+        if outer < OUTER - 1:
+            for y in range(ny):
+                MG[last, y] = precondition(G[last, y], y)
+            offers.append((last, offer(last)))
         rest = red.at[outer, pl.ds(0, count - 1)]
         pltpu.make_async_copy(rest, rest, recv_r.at[outer]).wait()
-        pltpu.make_async_copy(rest, rest, send_r.at[outer]).wait()
         total = jnp.sum(red[outer], axis=0)
-        low = jnp.sum(jnp.where(lane < half, total, 0.0), axis=1, keepdims=True)
-        high = jnp.sum(jnp.where(lane < half, 0.0, total), axis=1, keepdims=True)
+        column = jnp.sum(jnp.where(group == lane_16, total, 0.0), axis=1, keepdims=True)
         sums = {}
         for n, key in enumerate(order):
-            column = low if n < 8 else high
-            sums[key] = jnp.broadcast_to(column[n % 8 : n % 8 + 1], (8, nx))
+            sums[key] = jnp.broadcast_to(column[n : n + 1], (8, nx))
         gram = [[sums[min(i, j), max(i, j)] for j in range(ITERS)] for i in range(ITERS)]
         weights = solve(gram, [sums["r", i] for i in range(ITERS)])
         wide_weights = [jnp.broadcast_to(c[0:1], (levels, nx)) for c in weights]
 
-        for i in range(ITERS):
-            k = 1 + outer * ITERS + i
-            p_packed += weights[i] * packs[i]
-            p_south += wide_weights[i] * hs[k - 1]
-            p_north += wide_weights[i] * hn[k]
-        for y in range(ny):
-            value = prs[y]
-            for i in range(ITERS):
-                value += wide_weights[i] * W[i, y]
-            prs[y] = value
-        for y in range(ny):
-            value = prs[y]
-            edge = spread(p_packed, y)
-            to_east = jnp.where(lane_l == nx - 1, edge, roll_e(value))
-            to_north = prs[y + 1] if y < ny - 1 else p_north
-            fe[y] = fe[y] + ce[y] * (value - to_east)
-            fn[y] = fn[y] + cn[y] * (value - to_north)
-            if outer < OUTER - 1:
-                fwx[y] = fwx[y] + cw[y] * (edge - value)
-                if y == 0:
-                    fs[...] = fs[...] + cs[0] * (p_south - value)
-            else:
-                scatter(p_out, 0, y, value)
-                scatter(u_out, 0, y, sign[y : y + 1] * fe[y])
-                scatter(u_out, levels * ny, y, sign[ny + y : ny + y + 1] * fn[y])
+        late = (packs, souths, norths, weights, wide_weights)
+        if outer < OUTER - 1:
+            for y in range(ny):
+                W[start_w + ITERS, y] = combine(MG[ITERS, y], [MG[i, y] for i in range(ITERS)], wide_weights)
+                res[y] = combine(G[ITERS, y], [G[i, y] for i in range(ITERS)], wide_weights)
+            for term, copies in offers:
+                finish(copies)
+            offers = []
+            meets = [meet(gxw[i], gxe[i]) for i in range(ITERS + 1)]
+            started = (
+                combine(meets[ITERS], meets[:ITERS], weights),
+                combine(gs[ITERS], [gs[i] for i in range(ITERS)], wide_weights),
+                combine(gn[ITERS], [gn[i] for i in range(ITERS)], wide_weights),
+            )
+    update(OUTER - 1, *late, state)
+    for y in range(ny):
+        scatter(p_out, 0, y, prs[y])
+        scatter(u_out, 0, y, sign[y : y + 1] * fe[y])
+        scatter(u_out, levels * ny, y, sign[ny + y : ny + y + 1] * fn[y])
+    sent(first)
+    for copies in pending:
+        sent(copies)
+    for outer in range(OUTER):
+        rest = red.at[outer, pl.ds(0, count - 1)]
+        pltpu.make_async_copy(rest, rest, send_r.at[outer]).wait()
 
 
 def local(npx, npy, velocity, pressure, mass, face_coeff, vert_coeff, block_inverse, orientation):
@@ -371,15 +442,27 @@
     rounds = OUTER * ITERS
     field = pltpu.VMEM((ny, levels, nx), f32)
     slab = pltpu.VMEM((levels, nx), f32)
-    inputs = [a.reshape(-1, nx) for a in (velocity, pressure, mass, face_coeff, vert_coeff, block_inverse, orientation)]
+    flat = [a.reshape(-1, nx) for a in (velocity, pressure, mass, face_coeff, block_inverse, orientation)]
+    inputs = flat[:4] + [vert_coeff] + flat[4:]
+    names = ("vel_ref", "pres_ref", "mass_ref", "face_ref", "vert_ref", "inv_ref", "orient_ref")
     vmem = pl.BlockSpec(memory_space=pltpu.VMEM)
     scratch = dict(
-        wide=pltpu.VMEM((2 + BLOCK, levels * ny, nx), f32),
+        **{name: pltpu.VMEM(a.shape, a.dtype) for name, a in zip(names, inputs)},
+        wide=pltpu.VMEM((1 + BLOCK, levels * ny, nx), f32),
+        wide_w=pltpu.VMEM((levels, ny, nx), f32),
         mass=field, ce=field, cw=field, cn=field, cs=field, wu=field, wl=field, xc=field,
         binv=pltpu.VMEM((BLOCK, ny, levels, nx), f32),
-        prs=field, fe=field, fn=field, fwx=field, fs=slab, res=field,
-        W=pltpu.VMEM((ITERS, ny, levels, nx), f32),
+        prs=field, fe=field, fn=field, res=field,
+        G=pltpu.VMEM((ITERS + 1, ny, levels, nx), f32),
+        MG=pltpu.VMEM((ITERS + 1, ny, levels, nx), f32),
+        gs=pltpu.VMEM((ITERS + 1, levels, nx), f32),
+        gn=pltpu.VMEM((ITERS + 1, levels, nx), f32),
+        gpk=pltpu.VMEM((ITERS + 1, 8, nx), f32),
+        gxw=pltpu.VMEM((ITERS + 1, 8, nx), f32),
+        gxe=pltpu.VMEM((ITERS + 1, 8, nx), f32),
+        W=pltpu.VMEM((OUTER * ITERS, ny, levels, nx), f32),
         V=pltpu.VMEM((ITERS, ny, levels, nx), f32),
+        low_p=slab,
         seam=pltpu.VMEM((3, levels, nx), f32),
         hs=pltpu.VMEM((rounds, levels, nx), f32),
         hn=pltpu.VMEM((rounds + 1, levels, nx), f32),
@@ -389,13 +472,14 @@
         xe=pltpu.VMEM((rounds + 1, 8, nx), f32),
         pk0=pltpu.VMEM((3, 8, nx), f32),
         xw0=pltpu.VMEM((3, 8, nx), f32),
-        red=pltpu.VMEM((OUTER, npx * npy, 8, nx), f32),
-        send_y=pltpu.SemaphoreType.DMA((rounds + 1, 2)),
-        recv_y=pltpu.SemaphoreType.DMA((rounds + 1, 2)),
-        send_x=pltpu.SemaphoreType.DMA((rounds + 1, 2)),
-        recv_x=pltpu.SemaphoreType.DMA((rounds + 1, 2)),
+        red=pltpu.VMEM((OUTER, npx * npy, 1, nx), f32),
+        send_y=pltpu.SemaphoreType.DMA((rounds + ITERS + 2, 2)),
+        recv_y=pltpu.SemaphoreType.DMA((rounds + ITERS + 2, 2)),
+        send_x=pltpu.SemaphoreType.DMA((rounds + ITERS + 2, 2)),
+        recv_x=pltpu.SemaphoreType.DMA((rounds + ITERS + 2, 2)),
         send_r=pltpu.SemaphoreType.DMA((OUTER,)),
         recv_r=pltpu.SemaphoreType.DMA((OUTER,)),
+        fetch=pltpu.SemaphoreType.DMA((7,)),
     )
     p_new, u_new = pl.pallas_call(
         functools.partial(kernel, npx, npy, ny, nb, nx),
@@ -403,11 +487,11 @@
             jax.ShapeDtypeStruct((levels * ny, nx), f32),
             jax.ShapeDtypeStruct((2 * levels * ny, nx), f32),
         ),
-        in_specs=[vmem] * 7,
+        in_specs=[pl.BlockSpec(memory_space=pltpu.HBM)] * 7,
         out_specs=(vmem, vmem),
         scratch_shapes=list(scratch.values()),
         compiler_params=pltpu.CompilerParams(
-            collective_id=0, has_side_effects=True, vmem_limit_bytes=40 * 1024 * 1024
+            collective_id=0, has_side_effects=True, vmem_limit_bytes=125 * 512 * 1024
         ),
     )(*inputs)
     return p_new.reshape(pressure.shape), u_new.reshape(velocity.shape)

time: 55.9 us -> 48.6 us (0.87)
  Pallas kernels: 49.1 us -> 45.5 us
  local copies, waits for them, and re-layouts: 5.92 us -> 2.32 us
    pallas_call x1, Pallas kernels: 49.1 us -> 45.5 us  [local(): pl.pallas_call(functools.partial(kernel, npx, npy, ny, nb, nx), out_shape...]
    unnamed x14 -> x4, local copies, waits for them, and re-layouts: 5.01 us -> 2.32 us
    reshape x1 -> x0, local copies, waits for them, and re-layouts: 0.92 us -> none  [local(): a.reshape(-1, nx)]
where the time goes in v2:
time: 48.6 us; the launch traced here: 48.5 us
  Pallas kernels  45.5 us (94%)
  local copies, waits for them, and re-layouts  2.32 us (5%)
  between operations  0.65 us (1%)
    pallas_call x1, Pallas kernels, local(): pl.pallas_call(functools.partial(kernel, npx, npy, ny, nb, nx), out_shape...  45.5 us
    unnamed x4, local copies, waits for them, and re-layouts  2.32 us

profile of v2, /device:TPU:0, one launch (start us, length us, event | category | flops | bytes accessed | tf_op | source)
XLA Modules:
  0.0 48.5 jit_solution(1690633777016853209)
XLA Ops:
  0.6 45.5 %shard_map.86 = (f32[256,128]{1,0:T(8,128)}, f32[512,128]{1,0:T(8,128)}) custom-call(f32[512,128]{1,0:T(8,128)} %bitcast.9, f32[256,128]{1,0:T(8,128)} %bitcast.12, bf16[256,128]{1,0:T(8,128)(2,1)} %bitcast.14, bf16[512,128]{1,0:T(8,128)(2,1)} %bitcast.13, bf16[63,4,128]{2,1,0:T(4,128)(2,1)} %vert_hbm.1, bf16[1024,128]{1,0:T(8,128)(2,1)} %bitcast.10, ...), custom_call_target="tpu_custom_call" | custom-call | tf_op jit(solution)/shard_map/pallas_call | solution.py:484
  46.1 0.0 copy-start
  46.1 1.6 %copy.11 = f32[64,4,128]{2,1,0:T(4,128)} copy(f32[64,4,128]{2,1,0:T(4,128)} %bitcast.11) | data formatting | bytes 262144
  47.8 0.0 copy-done
  47.8 0.7 %copy.12 = f32[2,64,4,128]{3,2,1,0:T(4,128)} copy(f32[2,64,4,128]{3,2,1,0:T(4,128)S(1)} %bitcast.8) | data formatting | bytes 524288
Async XLA Ops:
  46.1 1.6 %copy-start = (f32[512,128]{1,0:T(8,128)S(1)}, f32[512,128]{1,0:T(8,128)}, u32[]{:S(2)}) copy-start(f32[512,128]{1,0:T(8,128)} %get-tuple-element.5) | copy-start | bytes 786436

commit v3 on v2

--- a/solution.py
+++ b/solution.py
@@ -42,8 +42,8 @@
     p_out, u_out,
     vel_ref, pres_ref, mass_ref, face_ref, vert_ref, inv_ref, orient_ref,
     wide, wide_w, mass, ce, cw, cn, cs, wu, wl, xc, binv, prs, fe, fn, res, G, MG, gs, gn, gpk, gxw, gxe,
-    W, V, low_p, seam, hs, hn, hs0, pk, xw, xe, pk0, xw0, red,
-    send_y, recv_y, send_x, recv_x, send_r, recv_r, fetch,
+    W, V, low_p, seam, hs, hn, hs0, pk, xw, xe, pk0, xw0, red, edges, pkC, hnC, hsC, xwC, xeC, cornersC, xcH, ends, hnD, xeD, cornersD,
+    send_h, recv_h, send_r, recv_r, fetch,
 ):
     levels = BLOCK * nb
     tiles = levels // 8
@@ -125,63 +125,85 @@
     def roll_e(slab):
         return pltpu.roll(slab, nx - 1, axis=1)
 
+    def remote(src, dst, pair, target, sends=None, lands=None):
+        copy = pltpu.make_async_remote_copy(
+            src_ref=src, dst_ref=dst, send_sem=pair[0], recv_sem=pair[1],
+            device_id=target, device_id_type=MESH)
+        return copy, sends, lands
+
+    def sems(k, n):
+        return send_h.at[k, n], recv_h.at[k, n]
+
     def y_copies(low, high, low_dst, high_dst, k):
-        north = pltpu.make_async_remote_copy(
-            src_ref=high, dst_ref=high_dst, send_sem=send_y.at[k, 0], recv_sem=recv_y.at[k, 0],
-            device_id=(px, py + 1), device_id_type=MESH)
-        south = pltpu.make_async_remote_copy(
-            src_ref=low, dst_ref=low_dst, send_sem=send_y.at[k, 1], recv_sem=recv_y.at[k, 1],
-            device_id=(px, py - 1), device_id_type=MESH)
-        return north, south
+        return [
+            remote(high, high_dst, sems(k, 0), (px, py + 1), has_north, has_south),
+            remote(low, low_dst, sems(k, 1), (px, py - 1), has_south, has_north),
+        ]
 
     def x_copies(to_east, to_west, east_dst, west_dst, k):
-        a = pltpu.make_async_remote_copy(
-            src_ref=to_east, dst_ref=east_dst, send_sem=send_x.at[k, 0], recv_sem=recv_x.at[k, 0],
-            device_id=(east, py), device_id_type=MESH)
-        b = pltpu.make_async_remote_copy(
-            src_ref=to_west, dst_ref=west_dst, send_sem=send_x.at[k, 1], recv_sem=recv_x.at[k, 1],
-            device_id=(west, py), device_id_type=MESH)
-        return a, b
+        return [
+            remote(to_east, east_dst, sems(k, 2), (east, py)),
+            remote(to_west, west_dst, sems(k, 3), (west, py)),
+        ]
+
+    def corner_copies(src, dst, k):
+        return [
+            remote(src, dst.at[0], sems(k, 4), (east, py + 1), has_north, has_south),
+            remote(src, dst.at[1], sems(k, 5), (west, py + 1), has_north, has_south),
+            remote(src, dst.at[2], sems(k, 6), (east, py - 1), has_south, has_north),
+            remote(src, dst.at[3], sems(k, 7), (west, py - 1), has_south, has_north),
+        ]
+
+    def under(condition, action):
+        if condition is None:
+            action()
+        else:
+            pl.when(condition)(action)
 
     def start(copies):
-        (north, south), (a, b) = copies
-
-        @pl.when(has_north)
-        def _():
-            north.start()
-
-        @pl.when(has_south)
-        def _():
-            south.start()
-
-        a.start()
-        b.start()
+        for copy, sends, _ in copies:
+            under(sends, copy.start)
 
     def finish(copies):
-        (north, south), (a, b) = copies
-        a.wait_recv()
-        b.wait_recv()
-
-        @pl.when(has_south)
-        def _():
-            north.wait_recv()
-
-        @pl.when(has_north)
-        def _():
-            south.wait_recv()
+        for copy, _, lands in copies:
+            under(lands, copy.wait_recv)
 
     def sent(copies):
-        (north, south), (a, b) = copies
-        a.wait_send()
-        b.wait_send()
-
-        @pl.when(has_north)
-        def _():
-            north.wait_send()
-
-        @pl.when(has_south)
-        def _():
-            south.wait_send()
+        for copy, sends, _ in copies:
+            under(sends, copy.wait_send)
+
+    place = lax.div(lax.rem(lane + 1, nx), 2)
+    lane_row = lax.div(place, tiles)
+    member = lax.div(lax.rem(place, tiles), tiles // BLOCK)
+    reach = 2 * tiles * (ny - 1)
+
+    def corners(slots):
+        south = jnp.where(
+            even, pltpu.roll(slots[0], nx - reach + 1, axis=1), pltpu.roll(slots[1], nx - reach - 1, axis=1))
+        north = jnp.where(
+            even, pltpu.roll(slots[2], reach + 1, axis=1), pltpu.roll(slots[3], reach - 1, axis=1))
+        return jnp.where(lane_row == ny - 1, north, jnp.where(lane_row == 0, south, 0.0))
+
+    def precondition_packed(value):
+        step = 2 * (tiles // BLOCK)
+        turned = {
+            d: pltpu.roll(value, (step * d) % nx, axis=1) if d else value
+            for d in range(1 - BLOCK, BLOCK)
+        }
+        total = jnp.zeros_like(value)
+        for j in range(BLOCK):
+            brought = turned[-j]
+            for m in range(1, BLOCK):
+                brought = jnp.where(member == m, turned[m - j], brought)
+            total += meet(xwC[2 + j], xeC[2 + j]) * brought
+        return total
+
+    def precondition_rows(entries, blocks):
+        parts = []
+        for m in range(BLOCK):
+            rows = slice(m * nb, (m + 1) * nb)
+            parts.append(sum(entries[1 + j, rows] * blocks[j * nb : (j + 1) * nb] for j in range(BLOCK)))
+        return jnp.concatenate(parts, axis=0)
 
     for copy in fetches[:4]:
         copy.wait()
@@ -206,19 +228,23 @@
     def _():
         hs0[...] = jnp.zeros_like(hs0)
         hs[...] = jnp.zeros_like(hs)
+        hsC[...] = jnp.zeros_like(hsC)
+        cornersC[0:2] = jnp.zeros_like(cornersC[0:2])
+        cornersD[:, 0:2] = jnp.zeros_like(cornersD[:, 0:2])
         gs[...] = jnp.zeros_like(gs)
 
     @pl.when(jnp.logical_not(has_north))
     def _():
         hn[...] = jnp.zeros_like(hn)
+        hnD[...] = jnp.zeros_like(hnD)
+        hnC[...] = jnp.zeros_like(hnC)
+        cornersC[2:4] = jnp.zeros_like(cornersC[2:4])
+        cornersD[:, 2:4] = jnp.zeros_like(cornersD[:, 2:4])
         gn[...] = jnp.zeros_like(gn)
 
     pl.semaphore_wait(barrier, count - 1)
 
-    first = (
-        y_copies(low_p, seam, hn.at[0], hs0, 0),
-        x_copies(pk0, pk0.at[0], xw0, xe.at[0], 0),
-    )
+    first = y_copies(low_p, seam, hn.at[0], hs0, 0) + x_copies(pk0, pk0.at[0], xw0, xe.at[0], 0)
     start(first)
 
     for copy in fetches[4:]:
@@ -238,6 +264,16 @@
         for j in range(BLOCK):
             binv[j, y] = gather(wide.at[1 + j], 0, y)
 
+    edges[0, 0], edges[1, 0] = ce[0], ce[ny - 1]
+    pkC[0], pkC[1] = pk0[2], pack(cn)
+    for j in range(BLOCK):
+        edges[0, 1 + j], edges[1, 1 + j] = binv[j, 0], binv[j, ny - 1]
+        pkC[2 + j] = pack(binv.at[j])
+    beyond = 2 + OUTER * ITERS + ITERS
+    fixed = y_copies(edges.at[0], edges.at[1], hnC, hsC, beyond)
+    fixed += x_copies(pkC, pkC, xwC, xeC, beyond)
+    fixed += corner_copies(pkC.at[pl.ds(0, 2)], cornersC, beyond)
+    start(fixed)
     finish(first)
     packed_c = meet(xw0[2], xw0[2])
     packed_f = meet(xw0[1], xw0[1])
@@ -288,10 +324,8 @@
     def offer(n):
         gpk[n] = pack([MG[n, y] for y in range(ny)])
         k = 1 + OUTER * ITERS + n
-        copies = (
-            y_copies(MG.at[n, 0], MG.at[n, ny - 1], gn.at[n], gs.at[n], k),
-            x_copies(gpk.at[n], gpk.at[n], gxw.at[n], gxe.at[n], k),
-        )
+        copies = y_copies(MG.at[n, 0], MG.at[n, ny - 1], gn.at[n], gs.at[n], k)
+        copies += x_copies(gpk.at[n], gpk.at[n], gxw.at[n], gxe.at[n], k)
         start(copies)
         pending.append(copies)
         return copies
@@ -334,38 +368,82 @@
         start_w = outer * ITERS
         packs, souths, norths = [], [], []
         dots = {}
+        todo, terms = [], [ITERS] if outer < OUTER - 1 else []
+        derived = started if outer > 0 else None
+
+        def products(i):
+            for j in range(i + 1):
+                dots[j, i] = sum(fold(V[j, y] * V[i, y]) for y in range(ny))
+            dots["r", i] = sum(fold(res[y] * V[i, y]) for y in range(ny))
+
         for i in range(ITERS):
             k = 1 + outer * ITERS + i
-            ready = outer > 0 and i == 0
-            if not ready:
-                pk[k - 1] = pack([W[start_w + i, y] for y in range(ny)])
-                copies = (
-                    y_copies(W.at[start_w + i, 0], W.at[start_w + i, ny - 1], hn.at[k], hs.at[k - 1], k),
-                    x_copies(pk.at[k - 1], pk.at[k - 1], xw.at[k - 1], xe.at[k], k),
-                )
+            here = W.at[start_w + i]
+            fresh = derived is None
+            double = fresh and i < ITERS - 1
+            if fresh:
+                own = pack([here[y] for y in range(ny)])
+                pk[k - 1, 0] = own
+            if fresh and not double:
+                copies = y_copies(here.at[0], here.at[ny - 1], hn.at[k], hs.at[k - 1, 0], k)
+                copies += x_copies(pk.at[k - 1, 0], pk.at[k - 1, 0], xw.at[k - 1, 0], xe.at[k], k)
                 start(copies)
-                pending.append(copies)
             for y in range(ny):
-                flat, image = inside(W.at[start_w + i], y)
+                flat, image = inside(here, y)
                 V[i, y] = image
                 if outer < OUTER - 1:
-                    G[i, y] = mass[y] * W[start_w + i, y] - flat - image
-            if i > 0:
-                for j in range(i):
-                    dots[j, i - 1] = sum(fold(V[j, y] * V[i - 1, y]) for y in range(ny))
-                dots["r", i - 1] = sum(fold(res[y] * V[i - 1, y]) for y in range(ny))
-            if outer < OUTER - 1:
-                term = (i - 1) % (ITERS + 1)
+                    G[i, y] = mass[y] * here[y] - flat - image
+            if double:
                 for y in range(ny):
-                    MG[term, y] = precondition(G[term, y], y)
-                offers.append((term, offer(term)))
-            if outer > 0 and i == 1:
-                state = update(outer - 1, *late, state)
-            if ready:
-                packed, south, north = started
+                    W[start_w + i + 1, y] = precondition(V[i, y], y) - SHIFT * here[y]
+                ahead = W.at[start_w + i + 1]
+                pk[k - 1, 1] = pack([ahead[y] for y in range(ny)])
+                for n, y in enumerate((0, ny - 1)):
+                    ends[k - 1, n, 0], ends[k - 1, n, 1] = here[y], ahead[y]
+                copies = y_copies(ends.at[k - 1, 0], ends.at[k - 1, 1], hnD.at[k - 1], hs.at[k - 1], k)
+                copies += x_copies(pk.at[k - 1], pk.at[k - 1], xw.at[k - 1], xeD.at[k - 1], k)
+                copies += corner_copies(pk.at[k - 1, 0], cornersD.at[k - 1], k)
+                start(copies)
+            if fresh:
+                pending.append(copies)
+                for n in todo:
+                    products(n)
+                todo = []
+                for n in terms:
+                    for y in range(ny):
+                        MG[n, y] = precondition(G[n, y], y)
+                    offers.append((n, offer(n)))
+                terms = []
+                if late is not None:
+                    state = update(outer - 1, *late, state)
+                    late = None
+                finish(copies)
+                south = hs[k - 1, 0]
+                north = hnD[k - 1, 0] if double else hn[k]
+                packed = meet(xw[k - 1, 0], xeD[k - 1, 0] if double else xe[k])
             else:
-                finish(copies)
-                packed, south, north = meet(xw[k - 1], xe[k]), hs[k - 1], hn[k]
+                packed, south, north = derived
+            derived = None
+            if double:
+                if fixed is not None:
+                    finish(fixed)
+                    pending.append(fixed)
+                    fixed = None
+                    coef = corners([cornersC[n, 0] for n in range(4)])
+                    for n, entries, row in ((0, hsC, 0), (1, hnC, ny - 1)):
+                        xcH[n] = jnp.where(
+                            lane_l == 0, spread(coef, row), jnp.where(lane_l == nx - 1, entries[0], 0.0))
+                    inner = jnp.where(even, packed_c, pk0[2])
+                    outward = jnp.where(
+                        lane_row == 0, corners([cornersC[n, 1] for n in range(4)]),
+                        jnp.where(lane_row == ny - 1, meet(xwC[1], xeC[1]), 0.0))
+                corner = corners([cornersD[k - 1, n] for n in range(4)])
+                derived = (
+                    meet(xw[k - 1, 1], xeD[k - 1, 1]) - precondition_packed(inner * own + outward * corner),
+                    hs[k - 1, 1] - precondition_rows(hsC, xcH[0] * spread(corner, 0) + cs[0] * here[0]),
+                    hnD[k - 1, 1] - precondition_rows(
+                        hnC, xcH[1] * spread(corner, ny - 1) + cn[ny - 1] * here[ny - 1]),
+                )
             packs.append(packed)
             souths.append(south)
             norths.append(north)
@@ -374,13 +452,14 @@
                 image = V[i, y] - border
                 V[i, y] = image
                 if i < ITERS - 1:
-                    W[start_w + i + 1, y] = precondition(image, y) - SHIFT * W[start_w + i, y]
+                    W[start_w + i + 1, y] = precondition(image, y) - SHIFT * here[y]
                 if outer < OUTER - 1:
                     G[i, y] = G[i, y] + 2.0 * border
-        last = ITERS - 1
-        for j in range(ITERS):
-            dots[j, last] = sum(fold(V[j, y] * V[last, y]) for y in range(ny))
-        dots["r", last] = sum(fold(res[y] * V[last, y]) for y in range(ny))
+            todo.append(i)
+            if outer < OUTER - 1:
+                terms.append(i)
+        for n in todo:
+            products(n)
 
         order = [(j, i) for i in range(ITERS) for j in range(i + 1)]
         order += [("r", i) for i in range(ITERS)]
@@ -394,9 +473,10 @@
                 send_sem=send_r.at[outer], recv_sem=recv_r.at[outer],
                 device_id=target, device_id_type=MESH).start()
         if outer < OUTER - 1:
-            for y in range(ny):
-                MG[last, y] = precondition(G[last, y], y)
-            offers.append((last, offer(last)))
+            for n in terms:
+                for y in range(ny):
+                    MG[n, y] = precondition(G[n, y], y)
+                offers.append((n, offer(n)))
         rest = red.at[outer, pl.ds(0, count - 1)]
         pltpu.make_async_copy(rest, rest, recv_r.at[outer]).wait()
         total = jnp.sum(red[outer], axis=0)
@@ -464,19 +544,29 @@
         V=pltpu.VMEM((ITERS, ny, levels, nx), f32),
         low_p=slab,
         seam=pltpu.VMEM((3, levels, nx), f32),
-        hs=pltpu.VMEM((rounds, levels, nx), f32),
+        hs=pltpu.VMEM((rounds, 2, levels, nx), f32),
         hn=pltpu.VMEM((rounds + 1, levels, nx), f32),
         hs0=pltpu.VMEM((3, levels, nx), f32),
-        pk=pltpu.VMEM((rounds, 8, nx), f32),
-        xw=pltpu.VMEM((rounds, 8, nx), f32),
+        pk=pltpu.VMEM((rounds, 2, 8, nx), f32),
+        xw=pltpu.VMEM((rounds, 2, 8, nx), f32),
         xe=pltpu.VMEM((rounds + 1, 8, nx), f32),
         pk0=pltpu.VMEM((3, 8, nx), f32),
         xw0=pltpu.VMEM((3, 8, nx), f32),
         red=pltpu.VMEM((OUTER, npx * npy, 1, nx), f32),
-        send_y=pltpu.SemaphoreType.DMA((rounds + ITERS + 2, 2)),
-        recv_y=pltpu.SemaphoreType.DMA((rounds + ITERS + 2, 2)),
-        send_x=pltpu.SemaphoreType.DMA((rounds + ITERS + 2, 2)),
-        recv_x=pltpu.SemaphoreType.DMA((rounds + ITERS + 2, 2)),
+        edges=pltpu.VMEM((2, 1 + BLOCK, levels, nx), f32),
+        pkC=pltpu.VMEM((2 + BLOCK, 8, nx), f32),
+        hnC=pltpu.VMEM((1 + BLOCK, levels, nx), f32),
+        hsC=pltpu.VMEM((1 + BLOCK, levels, nx), f32),
+        xwC=pltpu.VMEM((2 + BLOCK, 8, nx), f32),
+        xeC=pltpu.VMEM((2 + BLOCK, 8, nx), f32),
+        cornersC=pltpu.VMEM((4, 2, 8, nx), f32),
+        xcH=pltpu.VMEM((2, levels, nx), f32),
+        ends=pltpu.VMEM((rounds, 2, 2, levels, nx), f32),
+        hnD=pltpu.VMEM((rounds, 2, levels, nx), f32),
+        xeD=pltpu.VMEM((rounds, 2, 8, nx), f32),
+        cornersD=pltpu.VMEM((rounds, 4, 8, nx), f32),
+        send_h=pltpu.SemaphoreType.DMA((rounds + ITERS + 3, 8)),
+        recv_h=pltpu.SemaphoreType.DMA((rounds + ITERS + 3, 8)),
         send_r=pltpu.SemaphoreType.DMA((OUTER,)),
         recv_r=pltpu.SemaphoreType.DMA((OUTER,)),
         fetch=pltpu.SemaphoreType.DMA((7,)),

time: 48.6 us -> 46.2 us (0.951)
  Pallas kernels: 45.5 us -> 43.1 us
    pallas_call x1, Pallas kernels: 45.5 us -> 43.1 us  [local(): pl.pallas_call(functools.partial(kernel, npx, npy, ny, nb, nx), out_shape...]
where the time goes in v3:
time: 46.2 us; the launch traced here: 46 us
  Pallas kernels  43.1 us (93%)
  local copies, waits for them, and re-layouts  2.32 us (5%)
  between operations  0.65 us (1%)
    pallas_call x1, Pallas kernels, local(): pl.pallas_call(functools.partial(kernel, npx, npy, ny, nb, nx), out_shape...  43.1 us
    unnamed x4, local copies, waits for them, and re-layouts  2.32 us

profile of v3, /device:TPU:0, one launch (start us, length us, event | category | flops | bytes accessed | tf_op | source)
XLA Modules:
  0.0 46.0 jit_solution(12040348614697588617)
XLA Ops:
  0.6 43.1 %shard_map.86 = (f32[256,128]{1,0:T(8,128)}, f32[512,128]{1,0:T(8,128)}) custom-call(f32[512,128]{1,0:T(8,128)} %bitcast.9, f32[256,128]{1,0:T(8,128)} %bitcast.12, bf16[256,128]{1,0:T(8,128)(2,1)} %bitcast.14, bf16[512,128]{1,0:T(8,128)(2,1)} %bitcast.13, bf16[63,4,128]{2,1,0:T(4,128)(2,1)} %vert_hbm.1, bf16[1024,128]{1,0:T(8,128)(2,1)} %bitcast.10, ...), custom_call_target="tpu_custom_call" | custom-call | tf_op jit(solution)/shard_map/pallas_call | solution.py:574
  43.7 0.0 copy-start
  43.7 1.6 %copy.11 = f32[64,4,128]{2,1,0:T(4,128)} copy(f32[64,4,128]{2,1,0:T(4,128)} %bitcast.11) | data formatting | bytes 262144
  45.3 0.0 copy-done
  45.3 0.7 %copy.12 = f32[2,64,4,128]{3,2,1,0:T(4,128)} copy(f32[2,64,4,128]{3,2,1,0:T(4,128)S(1)} %bitcast.8) | data formatting | bytes 524288
Async XLA Ops:
  43.7 1.6 %copy-start = (f32[512,128]{1,0:T(8,128)S(1)}, f32[512,128]{1,0:T(8,128)}, u32[]{:S(2)}) copy-start(f32[512,128]{1,0:T(8,128)} %get-tuple-element.5) | copy-start | bytes 786436
